TPU v7x, 512 devices: a whole 4x8x8 slice. The times are simulated.
512 devices in a mesh: src: 16 (over y, z_hi), tgt: 32 (over z_lo, x, core).
Axes of the slice: x: 4, y: 8, z: 8 (z_hi: 2, z_lo: 4; z = z_hi * 4 + z_lo), core: 2. Of those that a mesh axis runs over, the one named last changes fastest.
Arguments:
- source_points: float32 [4096, 384], P('src'), as said below
- target_points: float32 [24576, 384], P('tgt'), as said below
- plan_start: float32 [4096, 24576], P('src', 'tgt'), may hold values from 0.06 to 140, as said below
- source_mass: float32 [4096], P('src'), may hold values from 0.3 to 3
- target_mass: float32 [24576], P('tgt'), may hold values from 0.3 to 3
- epsilon: float32 [1], replicated, may hold values from 0.5 to 1
Outputs:
- transported: float32 [4096, 384], P(('src', 'tgt'))
- core: float32 [384, 384], replicated
- column_scale: float32 [24576], P('tgt')
Inputs may be any that keep to these rules, and one draw needn't show every extreme that they name: `source_points`: real-valued features. `target_points`: real-valued features. `plan_start`: positive entries.
All inputs are finite; a program needn't handle non-finite values.
Results may differ from a plain program's by a relative error of at most 0.00011.
Values sent between devices are 32-bit elements; how exact they have to be, the bound alone decides.
A program may use at most 64 MiB of HBM per device.

v0:
```python
import jax
import jax.numpy as jnp
from jax import lax
from jax.sharding import Mesh
from jax.sharding import PartitionSpec as P

ITERS = 2
TGT = ("tgt_0", "tgt_1", "tgt_2")
SRC_TGT = ("src", "tgt_0", "tgt_1", "tgt_2")


def copy_for_each(array, axis):
    length = lax.axis_size(axis)
    return lax.all_to_all(
        jnp.broadcast_to(array[None], (length, *array.shape)), axis, 0, 0, tiled=True
    )


def taken_together(array, axis):
    everything = copy_for_each(array, axis)
    return jnp.sum(everything, axis=0)


def in_blocks(array, dim, length):
    before, after = (array.shape[:dim], array.shape[dim + 1 :])
    return jnp.moveaxis(array.reshape(*before, length, -1, *after), dim, 0)


def summed_on_arrival(array, axis, dim):
    blocks = in_blocks(array, dim, lax.axis_size(axis))
    arrived = lax.all_to_all(blocks, axis, split_axis=0, concat_axis=0, tiled=True)
    return arrived.sum(axis=0)


def sum_in_two_steps(array, axes, dim):
    far, near = axes
    own = summed_on_arrival(in_blocks(array, dim, lax.axis_size(far)), near, dim + 1)
    return jnp.sum(lax.all_to_all(own, far, 0, 0, tiled=True), axis=0)


def product(left, right):
    return jnp.dot(left, right, precision=lax.Precision.HIGHEST, preferred_element_type=jnp.float32)


def per_device(source_points, target_points, plan_start, source_mass, target_mass, epsilon):
    total_items = (
        source_points.shape[0] * lax.axis_size("src") * target_points.shape[0] * lax.axis_size(TGT)
    )
    term = product(source_points.T, product(plan_start, target_points))
    core = lax.psum(term, SRC_TGT) / total_items
    affinity = product(product(source_points, core), target_points.T)
    kernel = plan_start * jnp.exp(2.0 * affinity / epsilon[0])
    column_scale = jnp.ones((target_points.shape[0],), jnp.float32)
    row_scale = jnp.ones((source_points.shape[0],), jnp.float32)
    for sweep in range(ITERS):
        row_total = taken_together(product(kernel, column_scale), TGT)
        row_scale = source_mass / row_total
        column_total = taken_together(product(row_scale, kernel), "src")
        column_scale = target_mass / column_total
    weighted = kernel * row_scale[:, None] * column_scale[None, :]
    transported = sum_in_two_steps(
        product(weighted, target_points) / source_mass[:, None], (("tgt_0", "tgt_1"), "tgt_2"), 0
    )
    return (transported, core, column_scale)


def solution(mesh):
    torus = Mesh(
        mesh.devices.reshape(mesh.shape["src"], 4, 4, 2), ("src", "tgt_0", "tgt_1", "tgt_2")
    )
    placed = (P("src", None), P(TGT, None), P("src", TGT), P("src"), P(TGT), P())
    return jax.shard_map(
        per_device,
        mesh=torus,
        in_specs=placed,
        out_specs=(P(SRC_TGT, None), P(), P(TGT)),
        check_vma=False,
    )
```

profile of v0, /device:TPU:1, one launch (start us, length us, event | category | flops | bytes accessed | tf_op | source)
XLA Modules:
  0.0 384.0 jit_solution(1477316285604052106)
XLA Ops:
  7.2 0.0 copy-start
  7.2 0.0 copy-start.2
  7.2 0.0 all-reduce.2.cloned.1.call-start
  7.2 1.2 copy-done
  8.4 2.6 fusion.11
  11.0 0.0 copy-done.2
  11.0 1.6 convolution_bitcast_fusion
  12.7 0.0 copy-start.3
  12.7 0.0 all-reduce.2.cloned.1.call-update
  13.4 276.0 %all-reduce.2.cloned.1.call-done = f32[384,384]{0,1:T(8,128)} async-done(((f32[384,384]{0,1:T(8,128)}), f32[384,384]{0,1:T(8,128)}) %all-reduce.2.cloned.1.call-update) | async-done | bytes 589840 | tf_op jit(solution)/shard_map/psum | solution.py:50
  289.4 1.9 fusion.10
  291.3 0.0 copy-done.3
  291.3 0.0 copy-start.6
  291.3 2.1 fusion.2
  293.4 0.0 copy-start.5
  293.5 0.7 fusion.7
  294.2 14.8 %all_to_all.34 = f32[32,1,256]{2,1,0:T(1,128)S(1)} all-to-all(f32[32,1,256]{2,1,0:T(1,128)S(1)} %broadcast_in_dim.11), channel_id=1, replica_groups=mesh['src'=16,'tgt_0'=4,'tgt_1'=4,'tgt_2'=2] {'tgt_0','tgt_1','tgt_2'}, dimensions={0} | all-to-all | bytes 65536 | tf_op jit(solution)/shard_map/all_to_all | solution.py:14
  309.0 0.1 reduce_sum.54
  309.0 0.0 copy-done.6
  309.0 0.5 convolution_reduce_fusion.1
  309.6 18.7 %all_to_all.35 = f32[16,1,768]{2,1,0:T(1,128)S(1)} all-to-all(f32[16,1,768]{2,1,0:T(1,128)S(1)} %broadcast_in_dim.12), channel_id=1, replica_groups=mesh['src'=16,'tgt_0'=4,'tgt_1'=4,'tgt_2'=2] {'src'}, dimensions={0} | all-to-all | bytes 98304 | tf_op jit(solution)/shard_map/all_to_all | solution.py:14
  328.3 0.0 copy-done.5
  328.4 0.7 fusion.12
  329.1 12.2 %all_to_all.36 = f32[32,1,256]{2,1,0:T(1,128)S(1)} all-to-all(f32[32,1,256]{2,1,0:T(1,128)S(1)} %broadcast_in_dim.13), channel_id=1, replica_groups=mesh['src'=16,'tgt_0'=4,'tgt_1'=4,'tgt_2'=2] {'tgt_0','tgt_1','tgt_2'}, dimensions={0} | all-to-all | bytes 65536 | tf_op jit(solution)/shard_map/all_to_all | solution.py:14
  341.3 0.1 reduce_sum.56
  341.4 0.5 convolution_reduce_fusion
  341.9 14.3 %all_to_all.37 = f32[16,1,768]{2,1,0:T(1,128)S(1)} all-to-all(f32[16,1,768]{2,1,0:T(1,128)S(1)} %broadcast_in_dim.14), channel_id=1, replica_groups=mesh['src'=16,'tgt_0'=4,'tgt_1'=4,'tgt_2'=2] {'src'}, dimensions={0} | all-to-all | bytes 98304 | tf_op jit(solution)/shard_map/all_to_all | solution.py:14
  356.2 0.0 copy-start.4
  356.2 1.5 convolution_divide_fusion
  357.8 0.0 copy-done.4
  357.8 0.0 copy-start.1
  357.8 5.4 %all_to_all.38 = f32[2,16,8,384]{3,2,1,0:T(8,128)S(1)} all-to-all(f32[2,16,8,384]{3,2,1,0:T(8,128)S(1)} %bitcast.27), channel_id=1, replica_groups=mesh['src'=16,'tgt_0'=4,'tgt_1'=4,'tgt_2'=2] {'tgt_2'}, dimensions={0} | all-to-all | bytes 786432 | tf_op jit(solution)/shard_map/all_to_all | solution.py:31
  363.2 0.7 reduce_sum.58
  363.9 3.5 all-to-all-start.5
  367.4 0.0 copy-done.1
  367.4 0.1 broadcast_multiply_fusion
  367.5 1.1 copy.19
  368.5 8.0 %all-to-all-done.5 = f32[16,8,384]{2,1,0:T(8,128)S(1)} async-done(((f32[16,8,384]{2,1,0:T(8,128)}), f32[16,8,384]{2,1,0:T(8,128)S(1)}, u32[]{:S(2)}, u32[]{:S(2)}) %all-to-all-start.5) | async-done | bytes 196640 | tf_op jit(solution)/shard_map/all_to_all | solution.py:38
  376.5 0.6 reduce_sum.59
  (12 shorter events, 0.3 us)
Async XLA Ops:
  7.2 1.3 copy-start
  7.2 3.9 %copy-start.2 = (f32[256,384]{1,0:T(8,128)S(1)}, f32[256,384]{1,0:T(8,128)}, u32[]{:S(2)}) copy-start(f32[256,384]{1,0:T(8,128)} %param.6) | copy-start | bytes 1179652
  7.2 282.2 %all-reduce.2.cloned.1.call-start = ((), (), s32[]{:S(2)}) async-start(), calls=%async_computation.6 | async-start | bytes 1179648 | tf_op jit(solution)/shard_map/psum | solution.py:50
  12.7 278.6 %copy-start.3 = (f32[256,768]{1,0:T(8,128)S(1)}, f32[256,768]{1,0:T(8,128)}, u32[]{:S(2)}) copy-start(f32[256,768]{1,0:T(8,128)} %param.8) | copy-start | bytes 2359300
  291.3 17.7 %copy-start.6 = (f32[256]{0:T(256)S(1)}, f32[256]{0:T(256)}, u32[]{:S(2)}) copy-start(f32[256]{0:T(256)} %param.9) | copy-start | bytes 3076
  293.4 34.9 %copy-start.5 = (f32[768]{0:T(1024)S(1)}, f32[768]{0:T(1024)}, u32[]{:S(2)}) copy-start(f32[768]{0:T(1024)} %param.10) | copy-start | bytes 9220
  356.2 1.5 copy-start.4
  357.8 9.6 %copy-start.1 = (f32[384,384]{0,1:T(8,128)S(1)}, f32[384,384]{0,1:T(8,128)}, u32[]{:S(2)}) copy-start(f32[384,384]{0,1:T(8,128)} %all-reduce.2.cloned.1.call-done) | copy-start | bytes 1769476
  363.9 12.7 %all-to-all-start.5 = ((f32[16,8,384]{2,1,0:T(8,128)}), f32[16,8,384]{2,1,0:T(8,128)S(1)}, u32[]{:S(2)}, u32[]{:S(2)}) async-start(f32[16,8,384]{2,1,0:T(8,128)} %reduce_sum.58), calls=%async_computation.5 | async-start | bytes 393216 | tf_op jit(solution)/shard_map/all_to_all | solution.py:38
Sparse Core Ops, SparseCore 0:
  13.6 275.7 all-reduce.1
where the time goes:
time: 384 us
  waiting for transfers between devices  284 us (74%)
  blocking collectives  65.3 us (17%)
  between operations  15 us (4%)
  matrix products  12.1 us (3%)
    psum x1, waiting for transfers between devices, per_device(): core = lax.psum(term, SRC_TGT) / total_items  276 us
    all_to_all x4, blocking collectives, copy_for_each(): lax.all_to_all(jnp.broadcast_to(array[None], (length, *array.shape)), axi...  59.9 us
    dot_general x9, matrix products, product(): jnp.dot(left, right, precision=lax.Precision.HIGHEST, preferred_element_t...  12.1 us
    all_to_all x1, waiting for transfers between devices, sum_in_two_steps(): return jnp.sum(lax.all_to_all(own, far, 0, 0, tiled=True), axis=0)  8.02 us
  transfers between devices with their start and end apart: 2, of which 2 were waited for; matrix products, arithmetic and copies ran while one was open for 0% of the time, Pallas kernels for 0%

commit v1 on v0

v1 whole, which is shorter than its diff:
```python
import functools

import jax
import jax.numpy as jnp
from jax import lax
from jax.experimental import pallas as pl
from jax.experimental.pallas import tpu as pltpu
from jax.sharding import PartitionSpec as P

MESH = pl.DeviceIdType.MESH
D = 384
ROWS = 256
COLS = 768
SLAB = 12
TOTAL = 4096 * 24576

PAIR = (0, 1)


def near_mask(d):
    return (((d >> 2) & 1) << 1, ((d & 3) << 1) | (((d >> 3) & 1) << 3))


def wide_mask(e):
    return (((e & 3) << 2) | ((e >> 3) & 1), ((e >> 2) & 1) << 4)


def place(s, t):
    return (t // 2 % 4, s // 2, (s % 2) * 4 + t // 8)


def ring(a, b, n):
    return min(abs(a - b), n - abs(a - b))


def hops(mask):
    most = 0
    for s in range(16):
        for t in range(32):
            a, b = place(s, t), place(s ^ mask[0], t ^ mask[1])
            most = max(most, ring(a[0], b[0], 4) + ring(a[1], b[1], 8) + ring(a[2], b[2], 8))
    return most


def far_first(masks):
    return sorted(range(1, len(masks)), key=lambda d: -hops(masks[d]))


NEAR = [near_mask(d) for d in range(16)]
WIDE = [wide_mask(d) for d in range(16)]
TGT = [(0, d) for d in range(32)]
SRC = [(d, 0) for d in range(16)]
TILE = [(0, 2 * d) for d in range(16)]
NEAR_ORDER, WIDE_ORDER, TGT_ORDER, SRC_ORDER, TILE_ORDER = map(far_first, (NEAR, WIDE, TGT, SRC, TILE))
GREET = sorted({PAIR, *NEAR[1:], *WIDE[1:], *TGT[1:], *SRC[1:]})


def bits_of(value, n):
    return [lax.rem(lax.div(value, 1 << k), 2) for k in range(n)]


def flipped(value, bits, mask):
    for k, bit in enumerate(bits):
        if (mask >> k) & 1:
            value = value + (1 << k) * (1 - 2 * bit)
    return value


def dot(a, b, contract=((1,), (0,))):
    return lax.dot_general(
        a, b, (contract, ((), ())), precision=lax.Precision.HIGHEST, preferred_element_type=jnp.float32
    )


def body(
    s_ref, t_ref, p_ref, a_ref, b_ref, eps_ref,
    out_ref, core_ref, col_ref,
    st, half, pair_in, acc, near_in, wide, gathered, kern, row_in, col_in, part, part_in, mine, last_in,
    send, recv,
):
    si, ti = lax.axis_index("src"), lax.axis_index("tgt")
    sb, tb = bits_of(si, 4), bits_of(ti, 5)
    core = tb[0]
    g = tb[1] + 2 * tb[2] + 4 * sb[1] + 8 * tb[3]
    gb = [tb[1], tb[2], sb[1], tb[3]]
    w = sb[2] + 2 * sb[3] + 4 * tb[4] + 8 * sb[0]
    tile = tb[1] + 2 * tb[2] + 4 * tb[3] + 8 * tb[4]
    tileb = tb[1:]

    def device(mask):
        return (flipped(si, sb, mask[0]), flipped(ti, tb, mask[1]))

    def copy(src, dst, k, mask):
        return pltpu.make_async_remote_copy(
            src, dst, send.at[k], recv.at[k], device_id=device(mask), device_id_type=MESH
        )

    def arrived(ref, k):
        copy(ref, ref, k, PAIR).wait_recv()

    def sent(ref, k):
        copy(ref, ref, k, PAIR).wait_send()

    barrier = pltpu.get_barrier_semaphore()
    for mask in GREET:
        pl.semaphore_signal(barrier, inc=1, device_id=device(mask), device_id_type=MESH)

    st[...] = s_ref[...].T
    moved = dot(p_ref[...], t_ref[...])
    for k, h in ((0, 1 - core), (1, core)):
        value = dot(st[pl.ds(pl.multiple_of(h * 192, 8), 192), :], moved)
        for q in range(16):
            half[k, q] = value[q * SLAB : (q + 1) * SLAB]
        if k == 0:
            pl.semaphore_wait(barrier, len(GREET))
            copy(half.at[0], pair_in, 0, PAIR).start()
    arrived(pair_in, 0)
    acc[...] = half[1] + pair_in[...]

    for d in NEAR_ORDER:
        copy(acc.at[flipped(g, gb, d)], near_in.at[d - 1], 1, NEAR[d]).start()
    arrived(near_in, 1)
    total = acc[g]
    for d in range(15):
        total = total + near_in[d]
    wide[w] = total

    for d in WIDE_ORDER:
        copy(wide.at[w], wide.at[w], 2, WIDE[d]).start()
    arrived(wide.at[pl.ds(0, 15)], 2)
    total = wide[0]
    for d in range(1, 16):
        total = total + wide[d]
    gathered[core, g] = total / TOTAL

    for d in NEAR_ORDER:
        copy(gathered.at[core, g], gathered.at[core, g], 3, NEAR[d]).start()
    arrived(gathered.at[0, pl.ds(0, 15)], 3)
    copy(gathered.at[core], gathered.at[core], 4, PAIR).start()
    arrived(gathered.at[0], 4)
    for q in range(32):
        core_ref[q * SLAB : (q + 1) * SLAB, :] = gathered[q // 16, q % 16]

    rate = 2.0 / eps_ref[0]
    left = dot(s_ref[...], core_ref[...]) * rate
    kern[...] = p_ref[...] * jnp.exp(dot(left, t_ref[...], ((1,), (1,))))

    def settle(x):
        x = x + pltpu.roll(x, 4, 0)
        x = x + pltpu.roll(x, 2, 0)
        return x + pltpu.roll(x, 1, 0)

    def row_total(scale, k, n):
        parts = None
        for j in range(COLS // 128):
            piece = kern[:, j * 128 : (j + 1) * 128]
            if scale is not None:
                piece = piece * scale[0:1, j * 128 : (j + 1) * 128]
            parts = piece if parts is None else parts + piece
        across = parts.T
        x = across[0:8]
        for j in range(1, 16):
            x = x + across[j * 8 : (j + 1) * 8]
        row_in[n, 0] = settle(x)[0:1]
        for d in TGT_ORDER:
            copy(row_in.at[n, 0], row_in.at[n, d], k, TGT[d]).start()
        arrived(row_in.at[n, pl.ds(0, 31)], k)
        x = row_in[n, 0]
        for d in range(1, 32):
            x = x + row_in[n, d]
        return x

    def col_total(k, n):
        x = kern[0:8, :] * down[0:8, 0:1] if n == 0 else kern[0:8, :]
        for j in range(1, 32):
            piece = kern[j * 8 : (j + 1) * 8, :]
            x = x + (piece * down[j * 8 : (j + 1) * 8, 0:1] if n == 0 else piece)
        col_in[n, si] = settle(x)[0:1]
        for d in SRC_ORDER:
            copy(col_in.at[n, si], col_in.at[n, si], k, SRC[d]).start()
        arrived(col_in.at[n, pl.ds(0, 15)], k)
        x = col_in[n, 0]
        for d in range(1, 16):
            x = x + col_in[n, d]
        return x

    scale = None
    for n in range(2):
        row = a_ref[...] / row_total(scale, 5 + 2 * n, n)
        down = jnp.broadcast_to(row, (128, ROWS)).T
        if n == 1:
            kern[...] = kern[...] * down[:, 0:1]
        scale = b_ref[...] / col_total(6 + 2 * n, n)
    col_ref[...] = scale[0:1]

    value = dot(kern[...] * scale[0:1], t_ref[...])
    for q in range(32):
        part[q % 2, q // 2] = value[q * 8 : (q + 1) * 8]
    copy(part.at[1 - core], part_in, 9, PAIR).start()
    arrived(part_in, 9)
    mine[...] = part[core] + part_in[...]
    for d in TILE_ORDER:
        copy(mine.at[flipped(tile, tileb, d)], last_in.at[d - 1], 10, TILE[d]).start()
    arrived(last_in, 10)
    total = mine[tile]
    for d in range(15):
        total = total + last_in[d]
    out_ref[...] = total

    sent(half.at[0], 0)
    sent(near_in, 1)
    sent(wide.at[pl.ds(0, 15)], 2)
    sent(gathered.at[0, pl.ds(0, 15)], 3)
    sent(gathered.at[0], 4)
    for n in range(2):
        sent(row_in.at[n, pl.ds(0, 31)], 5 + 2 * n)
        sent(col_in.at[n, pl.ds(0, 15)], 6 + 2 * n)
    sent(part_in, 9)
    sent(last_in, 10)


def per_device(source_points, target_points, plan_start, source_mass, target_mass, epsilon):
    f32 = jnp.float32
    vmem = pl.BlockSpec(memory_space=pltpu.VMEM)
    out, core, col = pl.pallas_call(
        body,
        out_shape=(
            jax.ShapeDtypeStruct((8, D), f32),
            jax.ShapeDtypeStruct((D, D), f32),
            jax.ShapeDtypeStruct((1, COLS), f32),
        ),
        in_specs=[vmem] * 5 + [pl.BlockSpec(memory_space=pltpu.SMEM)],
        out_specs=(vmem, vmem, vmem),
        scratch_shapes=[
            pltpu.VMEM((D, ROWS), f32),
            pltpu.VMEM((2, 16, SLAB, D), f32),
            pltpu.VMEM((16, SLAB, D), f32),
            pltpu.VMEM((16, SLAB, D), f32),
            pltpu.VMEM((15, SLAB, D), f32),
            pltpu.VMEM((16, SLAB, D), f32),
            pltpu.VMEM((2, 16, SLAB, D), f32),
            pltpu.VMEM((ROWS, COLS), f32),
            pltpu.VMEM((2, 32, 1, ROWS), f32),
            pltpu.VMEM((2, 16, 1, COLS), f32),
            pltpu.VMEM((2, 16, 8, D), f32),
            pltpu.VMEM((16, 8, D), f32),
            pltpu.VMEM((16, 8, D), f32),
            pltpu.VMEM((15, 8, D), f32),
            pltpu.SemaphoreType.DMA((11,)),
            pltpu.SemaphoreType.DMA((11,)),
        ],
        compiler_params=pltpu.CompilerParams(
            collective_id=0, has_side_effects=True, vmem_limit_bytes=48 * 2**20
        ),
    )(
        source_points, target_points, plan_start,
        source_mass.reshape(1, ROWS), target_mass.reshape(1, COLS), epsilon,
    )
    mass = lax.dynamic_slice(source_mass, (8 * lax.axis_index("tgt"),), (8,))
    return out / mass[:, None], core, col.reshape(COLS)


def solution(mesh):
    return jax.shard_map(
        per_device,
        mesh=mesh,
        in_specs=(P("src", None), P("tgt", None), P("src", "tgt"), P("src"), P("tgt"), P()),
        out_specs=(P(("src", "tgt"), None), P(), P("tgt")),
        check_vma=False,
    )
```

time: 384 us -> 90.3 us (0.24)
  waiting for transfers between devices: 284 us -> 0 us
  Pallas kernels: 0 us -> 81 us
  blocking collectives: 65.3 us -> 0 us
  between operations: 15 us -> 1.31 us
  matrix products: 12.1 us -> 0 us
  local copies, waits for them, and re-layouts: 2.45 us -> 6.33 us
    psum x1 -> x0, waiting for transfers between devices: 276 us -> none  [per_device(): core = lax.psum(term, SRC_TGT) / total_items]
    pallas_call x0 -> x1, Pallas kernels: none -> 81 us  [per_device(): pl.pallas_call(body, out_shape=(jax.ShapeDtypeStruct((8, D), f32), jax.Sh...]
    all_to_all x5 -> x0, blocking collectives: 65.3 us -> none  [the longest x4 59.9 us: copy_for_each(): lax.all_to_all(jnp.broadcast_to(array[None], (length, *array.shape)), axi...]
    dot_general x9 -> x0, matrix products: 12.1 us -> none  [product(): jnp.dot(left, right, precision=lax.Precision.HIGHEST, preferred_element_t...]
    all_to_all x1 -> x0, waiting for transfers between devices: 8.02 us -> none  [sum_in_two_steps(): return jnp.sum(lax.all_to_all(own, far, 0, 0, tiled=True), axis=0)]
  transfers between devices with their start and end apart: 2 -> 0, of which waited for: 2 -> 0; matrix products, arithmetic and copies ran while one was open for 0% -> 0% of each run, Pallas kernels for 0% -> 0%
where the time goes in v1:
time: 90.3 us; the launch traced here: 89.9 us
  Pallas kernels  81 us (90%)
  local copies, waits for them, and re-layouts  6.33 us (7%)
  between operations  1.31 us (1%)
  other arithmetic  1.28 us (1%)
    pallas_call x1, Pallas kernels, per_device(): pl.pallas_call(body, out_shape=(jax.ShapeDtypeStruct((8, D), f32), jax.Sh...  81 us
    unnamed x9, local copies, waits for them, and re-layouts  4.89 us

profile of v1, /device:TPU:1, one launch (start us, length us, event | category | flops | bytes accessed | tf_op | source)
XLA Modules:
  0.0 89.9 jit_solution(10297239752815447847)
XLA Ops:
  0.6 0.8 dynamic_slice.3
  1.4 0.7 reshape.17.b_ref
  2.7 0.0 copy-start
  2.7 1.3 %copy-done = f32[768,384]{1,0:T(8,128)S(1)} copy-done((f32[768,384]{1,0:T(8,128)S(1)}, f32[768,384]{1,0:T(8,128)}, u32[]{:S(2)}) %copy-start) | copy-done | bytes 1179672
  4.0 0.0 copy-start.1
  4.0 1.1 %copy-done.1 = f32[256,768]{1,0:T(8,128)S(1)} copy-done((f32[256,768]{1,0:T(8,128)S(1)}, f32[256,768]{1,0:T(8,128)}, u32[]{:S(2)}) %copy-start.1) | copy-done | bytes 786456
  5.1 0.0 copy-start.2
  5.1 1.0 %copy-done.2 = f32[256,384]{1,0:T(8,128)S(1)} copy-done((f32[256,384]{1,0:T(8,128)S(1)}, f32[256,384]{1,0:T(8,128)}, u32[]{:S(2)}) %copy-start.2) | copy-done | bytes 393240
  6.1 0.0 copy-start.3
  6.1 0.7 copy-done.3
  6.8 81.0 %shard_map.85 = (f32[8,384]{1,0:T(8,128)S(1)}, f32[384,384]{1,0:T(8,128)S(1)}, f32[1,768]{1,0:T(1,128)S(1)}) custom-call(f32[256,384]{1,0:T(8,128)S(1)} %copy-done.2, f32[768,384]{1,0:T(8,128)S(1)} %copy-done, f32[256,768]{1,0:T(8,128)S(1)} %copy-done.1, f32[1,256]{1,0:T(1,128)S(1)} %bitcast.1, f32[1,768]{1,0:T(1,128)S(1)} %reshape.17.b_ref, f32[1]{0:T(128)S(6)} %copy.10.eps_ref), custom_call_target="tpu_custom_call" | custom-call | tf_op jit(solution)/shard_map/pallas_call | solution.py:225
  87.9 0.7 broadcast_divide_fusion
  88.5 0.6 reduce
  89.1 0.8 copy.11
Async XLA Ops:
  2.7 1.3 %copy-start = (f32[768,384]{1,0:T(8,128)S(1)}, f32[768,384]{1,0:T(8,128)}, u32[]{:S(2)}) copy-start(f32[768,384]{1,0:T(8,128)} %t_ref.1) | copy-start | bytes 3538948
  4.0 1.1 %copy-start.1 = (f32[256,768]{1,0:T(8,128)S(1)}, f32[256,768]{1,0:T(8,128)}, u32[]{:S(2)}) copy-start(f32[256,768]{1,0:T(8,128)} %p_ref.1) | copy-start | bytes 2359300
  5.1 1.0 %copy-start.2 = (f32[256,384]{1,0:T(8,128)S(1)}, f32[256,384]{1,0:T(8,128)}, u32[]{:S(2)}) copy-start(f32[256,384]{1,0:T(8,128)} %s_ref.1) | copy-start | bytes 1179652
  6.1 0.7 copy-start.3

commit v2 on v1

v2 whole, which is shorter than its diff:
```python
import functools

import jax
import jax.numpy as jnp
from jax import lax
from jax.experimental import pallas as pl
from jax.experimental.pallas import tpu as pltpu
from jax.sharding import PartitionSpec as P

MESH = pl.DeviceIdType.MESH
D = 384
ROWS = 256
COLS = 768
SLAB = 12
TOTAL = 4096 * 24576

PAIR = (0, 1)


def near_mask(d):
    return (((d >> 2) & 1) << 1, ((d & 3) << 1) | (((d >> 3) & 1) << 3))


def wide_mask(e):
    return (((e & 3) << 2) | ((e >> 3) & 1), ((e >> 2) & 1) << 4)


def place(s, t):
    return (t // 2 % 4, s // 2, (s % 2) * 4 + t // 8)


def ring(a, b, n):
    return min(abs(a - b), n - abs(a - b))


def hops(mask):
    most = 0
    for s in range(16):
        for t in range(32):
            a, b = place(s, t), place(s ^ mask[0], t ^ mask[1])
            most = max(most, ring(a[0], b[0], 4) + ring(a[1], b[1], 8) + ring(a[2], b[2], 8))
    return most


def far_first(masks):
    return sorted(range(1, len(masks)), key=lambda d: -hops(masks[d]))


NEAR = [near_mask(d) for d in range(16)]
WIDE = [wide_mask(d) for d in range(16)]
TGT = [(0, d) for d in range(32)]
SRC = [(d, 0) for d in range(16)]
TILE = [(0, 2 * d) for d in range(16)]
NEAR_ORDER, WIDE_ORDER, TGT_ORDER, SRC_ORDER, TILE_ORDER = map(far_first, (NEAR, WIDE, TGT, SRC, TILE))
GREET = sorted({PAIR, *NEAR[1:], *WIDE[1:], *TGT[1:], *SRC[1:]})


def bits_of(value, n):
    return [lax.rem(lax.div(value, 1 << k), 2) for k in range(n)]


def flipped(value, bits, mask):
    for k, bit in enumerate(bits):
        if (mask >> k) & 1:
            value = value + (1 << k) * (1 - 2 * bit)
    return value


def pieces(x):
    high = x.astype(jnp.bfloat16)
    return high, (x - high.astype(jnp.float32)).astype(jnp.bfloat16)


def dot(a, b, contract=((1,), (0,))):
    def one(left, right):
        return lax.dot_general(left, right, (contract, ((), ())), preferred_element_type=jnp.float32)

    return one(a[0], b[0]) + (one(a[0], b[1]) + one(a[1], b[0]))


def body(
    s_hbm, t_hbm, p_hbm, a_hbm, b_hbm, eps_hbm,
    out_ref, core_ref, col_ref,
    s_ref, t_ref, p_ref, a_ref, b_ref, eps_ref,
    sth, stl, th, tl, half, pair_in, acc, near_in, wide, gathered, kern, adown, row_in, col_in, part, part_in, mine, last_in,
    load, send, recv,
):
    si, ti = lax.axis_index("src"), lax.axis_index("tgt")
    sb, tb = bits_of(si, 4), bits_of(ti, 5)
    core = tb[0]
    g = tb[1] + 2 * tb[2] + 4 * sb[1] + 8 * tb[3]
    gb = [tb[1], tb[2], sb[1], tb[3]]
    w = sb[2] + 2 * sb[3] + 4 * tb[4] + 8 * sb[0]
    tile = tb[1] + 2 * tb[2] + 4 * tb[3] + 8 * tb[4]
    tileb = tb[1:]
    pending = []

    def device(mask):
        return (flipped(si, sb, mask[0]), flipped(ti, tb, mask[1]))

    def copy(src, dst, k, mask):
        return pltpu.make_async_remote_copy(
            src, dst, send.at[k], recv.at[k], device_id=device(mask), device_id_type=MESH
        )

    def arrived(ref, k):
        copy(ref, ref, k, PAIR).wait_recv()
        pending.append((ref, k))

    loads = [
        pltpu.make_async_copy(src, dst, load.at[k])
        for k, (src, dst) in enumerate(
            (
                (s_hbm, s_ref), (t_hbm, t_ref), (p_hbm, p_ref),
                (a_hbm, a_ref), (b_hbm, b_ref), (eps_hbm, eps_ref),
            )
        )
    ]
    for one in loads:
        one.start()
    barrier = pltpu.get_barrier_semaphore()
    for mask in GREET:
        pl.semaphore_signal(barrier, inc=1, device_id=device(mask), device_id_type=MESH)

    def stages():
        loads[0].wait()
        sth[...], stl[...] = pieces(s_ref[...].T)
        loads[1].wait()
        loads[2].wait()
        th[...], tl[...] = pieces(t_ref[...])
        moved = pieces(dot(pieces(p_ref[...]), (th[...], tl[...])))
        for k, h in ((0, 1 - core), (1, core)):
            rows = pl.ds(pl.multiple_of(h * 192, 64), 192)
            value = dot((sth[rows, :], stl[rows, :]), moved)
            for q in range(16):
                half[k, q] = value[q * SLAB : (q + 1) * SLAB]
            if k == 0:
                yield 0
                pl.semaphore_wait(barrier, len(GREET))
                yield 1
                copy(half.at[0], pair_in, 0, PAIR).start()
        for k in (3, 4, 5):
            loads[k].wait()
        mass = a_ref[...].reshape(1, ROWS)
        target = b_ref[...].reshape(1, COLS)
        adown[...] = jnp.broadcast_to(mass, (128, ROWS)).T
        arrived(pair_in, 0)
        acc[...] = half[1] + pair_in[...]
        yield 2

        for d in NEAR_ORDER:
            copy(acc.at[flipped(g, gb, d)], near_in.at[d - 1], 1, NEAR[d]).start()
        arrived(near_in, 1)
        total = acc[g]
        for d in range(15):
            total = total + near_in[d]
        wide[w] = total
        yield 3

        for d in WIDE_ORDER:
            copy(wide.at[w], wide.at[w], 2, WIDE[d]).start()
        arrived(wide.at[pl.ds(0, 15)], 2)
        total = wide[0]
        for d in range(1, 16):
            total = total + wide[d]
        gathered[core, g] = total / TOTAL
        yield 4

        for d in NEAR_ORDER:
            copy(gathered.at[core, g], gathered.at[core, g], 3, NEAR[d]).start()
        arrived(gathered.at[0, pl.ds(0, 15)], 3)
        yield 5
        copy(gathered.at[core], gathered.at[core], 4, PAIR).start()

        def product_of(h):
            rows = pl.ds(pl.multiple_of(h * 192, 64), 192)
            block = jnp.concatenate([gathered[h, q] for q in range(16)], axis=0)
            core_ref[rows, :] = block
            return dot((sth[rows, :], stl[rows, :]), pieces(block), ((0,), (0,)))

        left = product_of(core)
        arrived(gathered.at[0], 4)
        left = (left + product_of(1 - core)) * (2.0 / eps_ref[0])
        yield 6

        kern[...] = p_ref[...] * jnp.exp(dot(pieces(left), (th[...], tl[...]), ((1,), (1,))))
        yield 7

        def settle(x):
            x = x + pltpu.roll(x, 4, 0)
            x = x + pltpu.roll(x, 2, 0)
            return x + pltpu.roll(x, 1, 0)

        def row_total(scale, k, n):
            parts = None
            for j in range(COLS // 128):
                piece = kern[:, j * 128 : (j + 1) * 128]
                if scale is not None:
                    piece = piece * scale[0:1, j * 128 : (j + 1) * 128]
                parts = piece if parts is None else parts + piece
            across = parts.T
            x = across[0:8]
            for j in range(1, 16):
                x = x + across[j * 8 : (j + 1) * 8]
            row_in[n, 0] = settle(x)[0:1]
            for d in TGT_ORDER:
                copy(row_in.at[n, 0], row_in.at[n, d], k, TGT[d]).start()
            arrived(row_in.at[n, pl.ds(0, 31)], k)
            x = row_in[n, 0]
            for d in range(1, 32):
                x = x + row_in[n, d]
            return x

        def col_total(down, k, n):
            pieces = []
            for j in range(COLS // 128):
                piece = kern[:, j * 128 : (j + 1) * 128] * down
                if n == 1:
                    kern[:, j * 128 : (j + 1) * 128] = piece
                x = piece[0:8]
                for i in range(1, 32):
                    x = x + piece[i * 8 : (i + 1) * 8]
                pieces.append(settle(x)[0:1])
            col_in[n, si] = jnp.concatenate(pieces, axis=1)
            for d in SRC_ORDER:
                copy(col_in.at[n, si], col_in.at[n, si], k, SRC[d]).start()
            arrived(col_in.at[n, pl.ds(0, 15)], k)
            x = col_in[n, 0]
            for d in range(1, 16):
                x = x + col_in[n, d]
            return x

        scale = None
        for n in range(2):
            row = mass / row_total(scale, 5 + 2 * n, n)
            yield 8 + 2 * n
            down = jnp.broadcast_to(row, (128, ROWS)).T
            scale = target / col_total(down, 6 + 2 * n, n)
            yield 9 + 2 * n
        col_ref[...] = scale.reshape(COLS)

        kern4 = kern.reshape(16, 2, 8, COLS)
        for k, h in ((0, 1 - core), (1, core)):
            block = kern4[:, h].reshape(128, COLS) * scale
            part[k] = dot(pieces(block), (th[...], tl[...])).reshape(16, 8, D)
            if k == 0:
                copy(part.at[0], part_in, 9, PAIR).start()
        arrived(part_in, 9)
        mine[...] = part[1] + part_in[...]
        yield 12
        for d in TILE_ORDER:
            copy(mine.at[flipped(tile, tileb, d)], last_in.at[d - 1], 10, TILE[d]).start()
        arrived(last_in, 10)
        total = mine[tile]
        for d in range(15):
            total = total + last_in[d]
        own = adown[pl.ds(pl.multiple_of(ti * 8, 8), 8), :]
        for j in range(D // 128):
            out_ref[:, j * 128 : (j + 1) * 128] = total[:, j * 128 : (j + 1) * 128] / own
        yield 13

    for at in stages():
        if at >= STAGE:
            break
    if STAGE < 1:
        pl.semaphore_wait(barrier, len(GREET))
    if STAGE < 2:
        for k in (3, 4, 5):
            loads[k].wait()
    if STAGE == 1:
        pass
    for ref, k in pending:
        copy(ref, ref, k, PAIR).wait_send()


def leave(out_in, core_in, col_in, out_ref, core_ref, col_ref, sem):
    copies = [
        pltpu.make_async_copy(src, dst, sem.at[k])
        for k, (src, dst) in enumerate(((core_in, core_ref), (out_in, out_ref), (col_in, col_ref)))
    ]
    for one in copies:
        one.start()
    for one in copies:
        one.wait()


STAGE = 99


def per_device(*args):
    f32 = jnp.float32
    vmem = pl.BlockSpec(memory_space=pltpu.VMEM)
    hbm = pl.BlockSpec(memory_space=pltpu.HBM)
    results = (
        jax.ShapeDtypeStruct((8, D), f32),
        jax.ShapeDtypeStruct((D, D), f32),
        jax.ShapeDtypeStruct((COLS,), f32),
    )
    out, core, col = pl.pallas_call(
        body,
        out_shape=results,
        in_specs=[hbm] * 6,
        out_specs=(vmem, vmem, vmem),
        scratch_shapes=[
            pltpu.VMEM((ROWS, D), f32),
            pltpu.VMEM((COLS, D), f32),
            pltpu.VMEM((ROWS, COLS), f32),
            pltpu.VMEM((ROWS,), f32),
            pltpu.VMEM((COLS,), f32),
            pltpu.SMEM((1,), f32),
            pltpu.VMEM((D, ROWS), jnp.bfloat16),
            pltpu.VMEM((D, ROWS), jnp.bfloat16),
            pltpu.VMEM((COLS, D), jnp.bfloat16),
            pltpu.VMEM((COLS, D), jnp.bfloat16),
            pltpu.VMEM((2, 16, SLAB, D), f32),
            pltpu.VMEM((16, SLAB, D), f32),
            pltpu.VMEM((16, SLAB, D), f32),
            pltpu.VMEM((15, SLAB, D), f32),
            pltpu.VMEM((16, SLAB, D), f32),
            pltpu.VMEM((2, 16, SLAB, D), f32),
            pltpu.VMEM((ROWS, COLS), f32),
            pltpu.VMEM((ROWS, 128), f32),
            pltpu.VMEM((2, 32, 1, ROWS), f32),
            pltpu.VMEM((2, 16, 1, COLS), f32),
            pltpu.VMEM((2, 16, 8, D), f32),
            pltpu.VMEM((16, 8, D), f32),
            pltpu.VMEM((16, 8, D), f32),
            pltpu.VMEM((15, 8, D), f32),
            pltpu.SemaphoreType.DMA((6,)),
            pltpu.SemaphoreType.DMA((11,)),
            pltpu.SemaphoreType.DMA((11,)),
        ],
        compiler_params=pltpu.CompilerParams(
            collective_id=0, has_side_effects=True, vmem_limit_bytes=60 * 2**20
        ),
    )(*args)
    out, core, col = pl.pallas_call(
        leave,
        out_shape=results,
        in_specs=[vmem] * 3,
        out_specs=(hbm, hbm, hbm),
        scratch_shapes=[pltpu.SemaphoreType.DMA((3,))],
    )(out, core, col)
    return out, core, col


def solution(mesh):
    return jax.shard_map(
        per_device,
        mesh=mesh,
        in_specs=(P("src", None), P("tgt", None), P("src", "tgt"), P("src"), P("tgt"), P()),
        out_specs=(P(("src", "tgt"), None), P(), P("tgt")),
        check_vma=False,
    )
```

time: 90.3 us -> 83.3 us (0.922)
  local copies, waits for them, and re-layouts: 6.33 us -> 0 us
  other arithmetic: 1.28 us -> 0 us
    unnamed x9 -> x0, local copies, waits for them, and re-layouts: 4.89 us -> none
    pallas_call x1 -> x2, Pallas kernels: 81 us -> 81.9 us  [the longest x1 80 us: per_device(): pl.pallas_call(body, out_shape=results, in_specs=[hbm] * 6, out_specs=(vm...]
where the time goes in v2:
time: 83.3 us; the launch traced here: 83.2 us
  Pallas kernels  81.9 us (98%)
  between operations  1.29 us (2%)
    pallas_call x1, Pallas kernels, per_device(): pl.pallas_call(body, out_shape=results, in_specs=[hbm] * 6, out_specs=(vm...  80 us
    pallas_call x1, Pallas kernels, per_device(): pl.pallas_call(leave, out_shape=results, in_specs=[vmem] * 3, out_specs=(...  1.91 us

profile of v2, /device:TPU:1, one launch (start us, length us, event | category | flops | bytes accessed | tf_op | source)
XLA Modules:
  0.0 83.2 jit_solution(2252439547384100575)
XLA Ops:
  1.3 80.0 %shard_map.85 = (f32[8,384]{1,0:T(8,128)}, f32[384,384]{1,0:T(8,128)}, f32[768]{0:T(1024)}) custom-call(f32[256,384]{1,0:T(8,128)} %s_hbm.1, f32[768,384]{1,0:T(8,128)} %t_hbm.1, f32[256,768]{1,0:T(8,128)} %p_hbm.1, f32[256]{0:T(256)} %a_hbm.1, f32[768]{0:T(1024)} %b_hbm.1, f32[1]{0:T(128)S(6)} %copy.9.eps_hbm), custom_call_target="tpu_custom_call" | custom-call | tf_op jit(solution)/shard_map/pallas_call | solution.py:299
  81.3 1.9 %shard_map.86 = (f32[8,384]{1,0:T(8,128)}, f32[384,384]{1,0:T(8,128)}, f32[768]{0:T(1024)}) custom-call(f32[8,384]{1,0:T(8,128)} %get-tuple-element.6.out_in, f32[384,384]{1,0:T(8,128)} %get-tuple-element.7.core_in, f32[768]{0:T(1024)} %get-tuple-element.8.col_in), custom_call_target="tpu_custom_call" | custom-call | tf_op jit(solution)/shard_map/pallas_call | solution.py:337

commit v3 on v2

--- a/solution.py
+++ b/solution.py
@@ -11,7 +11,8 @@
 D = 384
 ROWS = 256
 COLS = 768
-SLAB = 12
+SLAB = 36
+HALF = 192
 TOTAL = 4096 * 24576
 
 PAIR = (0, 1)
@@ -107,15 +108,13 @@
         copy(ref, ref, k, PAIR).wait_recv()
         pending.append((ref, k))
 
-    loads = [
-        pltpu.make_async_copy(src, dst, load.at[k])
-        for k, (src, dst) in enumerate(
-            (
-                (s_hbm, s_ref), (t_hbm, t_ref), (p_hbm, p_ref),
-                (a_hbm, a_ref), (b_hbm, b_ref), (eps_hbm, eps_ref),
-            )
-        )
-    ]
+    third = COLS // 3
+    ranges = []
+    for j in range(3):
+        some = pl.ds(j * third, third)
+        ranges += [(t_hbm.at[some, :], t_ref.at[some, :]), (p_hbm.at[:, some], p_ref.at[:, some])]
+    ranges += [(s_hbm, s_ref), (a_hbm, a_ref), (b_hbm, b_ref), (eps_hbm, eps_ref)]
+    loads = [pltpu.make_async_copy(src, dst, load.at[k]) for k, (src, dst) in enumerate(ranges)]
     for one in loads:
         one.start()
     barrier = pltpu.get_barrier_semaphore()
@@ -123,23 +122,29 @@
         pl.semaphore_signal(barrier, inc=1, device_id=device(mask), device_id_type=MESH)
 
     def stages():
-        loads[0].wait()
+        moved = None
+        for j in range(3):
+            loads[2 * j].wait()
+            loads[2 * j + 1].wait()
+            some = slice(j * third, (j + 1) * third)
+            th[some], tl[some] = pieces(t_ref[some])
+            term = dot(pieces(p_ref[:, some]), (th[some], tl[some]))
+            moved = term if moved is None else moved + term
+        loads[6].wait()
         sth[...], stl[...] = pieces(s_ref[...].T)
-        loads[1].wait()
-        loads[2].wait()
-        th[...], tl[...] = pieces(t_ref[...])
-        moved = pieces(dot(pieces(p_ref[...]), (th[...], tl[...])))
+        moved = pieces(moved)
         for k, h in ((0, 1 - core), (1, core)):
-            rows = pl.ds(pl.multiple_of(h * 192, 64), 192)
+            rows = pl.ds(pl.multiple_of(h * HALF, 64), HALF)
             value = dot((sth[rows, :], stl[rows, :]), moved)
+            flat = jnp.concatenate([value[:, j * 128 : (j + 1) * 128] for j in range(3)], axis=0)
             for q in range(16):
-                half[k, q] = value[q * SLAB : (q + 1) * SLAB]
+                half[k, q] = flat[q * SLAB : (q + 1) * SLAB]
             if k == 0:
                 yield 0
                 pl.semaphore_wait(barrier, len(GREET))
                 yield 1
                 copy(half.at[0], pair_in, 0, PAIR).start()
-        for k in (3, 4, 5):
+        for k in (7, 8, 9):
             loads[k].wait()
         mass = a_ref[...].reshape(1, ROWS)
         target = b_ref[...].reshape(1, COLS)
@@ -173,8 +178,9 @@
         copy(gathered.at[core], gathered.at[core], 4, PAIR).start()
 
         def product_of(h):
-            rows = pl.ds(pl.multiple_of(h * 192, 64), 192)
-            block = jnp.concatenate([gathered[h, q] for q in range(16)], axis=0)
+            rows = pl.ds(pl.multiple_of(h * HALF, 64), HALF)
+            flat = jnp.concatenate([gathered[h, q] for q in range(16)], axis=0)
+            block = jnp.concatenate([flat[j * HALF : (j + 1) * HALF] for j in range(3)], axis=1)
             core_ref[rows, :] = block
             return dot((sth[rows, :], stl[rows, :]), pieces(block), ((0,), (0,)))
 
@@ -265,10 +271,8 @@
     if STAGE < 1:
         pl.semaphore_wait(barrier, len(GREET))
     if STAGE < 2:
-        for k in (3, 4, 5):
+        for k in (7, 8, 9):
             loads[k].wait()
-    if STAGE == 1:
-        pass
     for ref, k in pending:
         copy(ref, ref, k, PAIR).wait_send()
 
@@ -312,12 +316,12 @@
             pltpu.VMEM((D, ROWS), jnp.bfloat16),
             pltpu.VMEM((COLS, D), jnp.bfloat16),
             pltpu.VMEM((COLS, D), jnp.bfloat16),
-            pltpu.VMEM((2, 16, SLAB, D), f32),
-            pltpu.VMEM((16, SLAB, D), f32),
-            pltpu.VMEM((16, SLAB, D), f32),
-            pltpu.VMEM((15, SLAB, D), f32),
-            pltpu.VMEM((16, SLAB, D), f32),
-            pltpu.VMEM((2, 16, SLAB, D), f32),
+            pltpu.VMEM((2, 16, SLAB, 128), f32),
+            pltpu.VMEM((16, SLAB, 128), f32),
+            pltpu.VMEM((16, SLAB, 128), f32),
+            pltpu.VMEM((15, SLAB, 128), f32),
+            pltpu.VMEM((16, SLAB, 128), f32),
+            pltpu.VMEM((2, 16, SLAB, 128), f32),
             pltpu.VMEM((ROWS, COLS), f32),
             pltpu.VMEM((ROWS, 128), f32),
             pltpu.VMEM((2, 32, 1, ROWS), f32),
@@ -326,7 +330,7 @@
             pltpu.VMEM((16, 8, D), f32),
             pltpu.VMEM((16, 8, D), f32),
             pltpu.VMEM((15, 8, D), f32),
-            pltpu.SemaphoreType.DMA((6,)),
+            pltpu.SemaphoreType.DMA((10,)),
             pltpu.SemaphoreType.DMA((11,)),
             pltpu.SemaphoreType.DMA((11,)),
         ],

time: 83.3 us -> 78.7 us (0.945)
  Pallas kernels: 81.9 us -> 77.2 us
    pallas_call x1, Pallas kernels: 80 us -> 75.3 us  [per_device(): pl.pallas_call(body, out_shape=results, in_specs=[hbm] * 6, out_specs=(vm...]
where the time goes in v3:
time: 78.7 us; the launch traced here: 78.5 us
  Pallas kernels  77.2 us (98%)
  between operations  1.29 us (2%)
    pallas_call x1, Pallas kernels, per_device(): pl.pallas_call(body, out_shape=results, in_specs=[hbm] * 6, out_specs=(vm...  75.3 us
    pallas_call x1, Pallas kernels, per_device(): pl.pallas_call(leave, out_shape=results, in_specs=[vmem] * 3, out_specs=(...  1.91 us

profile of v3, /device:TPU:1, one launch (start us, length us, event | category | flops | bytes accessed | tf_op | source)
XLA Modules:
  0.0 78.5 jit_solution(11075643470406215848)
XLA Ops:
  1.3 75.3 %shard_map.85 = (f32[8,384]{1,0:T(8,128)}, f32[384,384]{1,0:T(8,128)}, f32[768]{0:T(1024)}) custom-call(f32[256,384]{1,0:T(8,128)} %s_hbm.1, f32[768,384]{1,0:T(8,128)} %t_hbm.1, f32[256,768]{1,0:T(8,128)} %p_hbm.1, f32[256]{0:T(256)} %a_hbm.1, f32[768]{0:T(1024)} %b_hbm.1, f32[1]{0:T(128)S(6)} %copy.9.eps_hbm), custom_call_target="tpu_custom_call" | custom-call | tf_op jit(solution)/shard_map/pallas_call | solution.py:303
  76.6 1.9 %shard_map.86 = (f32[8,384]{1,0:T(8,128)}, f32[384,384]{1,0:T(8,128)}, f32[768]{0:T(1024)}) custom-call(f32[8,384]{1,0:T(8,128)} %get-tuple-element.6.out_in, f32[384,384]{1,0:T(8,128)} %get-tuple-element.7.core_in, f32[768]{0:T(1024)} %get-tuple-element.8.col_in), custom_call_target="tpu_custom_call" | custom-call | tf_op jit(solution)/shard_map/pallas_call | solution.py:341

commit v4 on v1

v4 whole, which is shorter than its diff:
```python
import functools

import jax
import jax.numpy as jnp
from jax import lax
from jax.experimental import pallas as pl
from jax.experimental.pallas import tpu as pltpu
from jax.sharding import PartitionSpec as P

MESH = pl.DeviceIdType.MESH
D = 384
ROWS = 256
COLS = 768
SLAB = 36
HALF = 192
TOTAL = 4096 * 24576

PAIR = (0, 1)


def near_mask(d):
    return (((d >> 2) & 1) << 1, ((d & 3) << 1) | (((d >> 3) & 1) << 3))


def wide_mask(e):
    return (((e & 3) << 2) | ((e >> 3) & 1), ((e >> 2) & 1) << 4)


def place(s, t):
    return (t // 2 % 4, s // 2, (s % 2) * 4 + t // 8)


def ring(a, b, n):
    return min(abs(a - b), n - abs(a - b))


def hops(mask):
    most = 0
    for s in range(16):
        for t in range(32):
            a, b = place(s, t), place(s ^ mask[0], t ^ mask[1])
            most = max(most, ring(a[0], b[0], 4) + ring(a[1], b[1], 8) + ring(a[2], b[2], 8))
    return most


def far_first(masks):
    return sorted(range(1, len(masks)), key=lambda d: -hops(masks[d]))


NEAR = [near_mask(d) for d in range(16)]
WIDE = [wide_mask(d) for d in range(16)]
TGT = [(0, d) for d in range(32)]
SRC = [(d, 0) for d in range(16)]
TILE = [(0, 2 * d) for d in range(16)]
NEAR_ORDER, WIDE_ORDER, TGT_ORDER, SRC_ORDER, TILE_ORDER = map(far_first, (NEAR, WIDE, TGT, SRC, TILE))
EARLY = [d for d in NEAR_ORDER if hops(NEAR[d]) <= 2]
LATE = [d for d in NEAR_ORDER if hops(NEAR[d]) > 2]
GREET = sorted({PAIR, *NEAR[1:], *WIDE[1:]})


def bits_of(value, n):
    return [lax.rem(lax.div(value, 1 << k), 2) for k in range(n)]


def flipped(value, bits, mask):
    for k, bit in enumerate(bits):
        if (mask >> k) & 1:
            value = value + (1 << k) * (1 - 2 * bit)
    return value


def pieces(x):
    high = x.astype(jnp.bfloat16)
    return high, (x - high.astype(jnp.float32)).astype(jnp.bfloat16)


def dot(a, b, contract=((1,), (0,))):
    def one(left, right):
        return lax.dot_general(left, right, (contract, ((), ())), preferred_element_type=jnp.float32)

    return one(a[0], b[0]) + (one(a[0], b[1]) + one(a[1], b[0]))


def body(
    s_hbm, t_hbm, p_hbm, a_hbm, b_hbm, eps_hbm,
    out_ref, core_hbm, col_hbm,
    core_ref, col_ref, s_ref, t_ref, p_ref, a_ref, b_ref, eps_ref,
    sth, stl, th, tl, half, pair_in, acc, near_in, wide, gathered, kern, adown, row_in, col_in, part, part_in, mine, last_in,
    load, send, recv,
):
    si, ti = lax.axis_index("src"), lax.axis_index("tgt")
    sb, tb = bits_of(si, 4), bits_of(ti, 5)
    core = tb[0]
    g = tb[1] + 2 * tb[2] + 4 * sb[1] + 8 * tb[3]
    gb = [tb[1], tb[2], sb[1], tb[3]]
    w = sb[2] + 2 * sb[3] + 4 * tb[4] + 8 * sb[0]
    tile = tb[1] + 2 * tb[2] + 4 * tb[3] + 8 * tb[4]
    tileb = tb[1:]
    pending = []

    def device(mask):
        return (flipped(si, sb, mask[0]), flipped(ti, tb, mask[1]))

    def copy(src, dst, k, mask):
        return pltpu.make_async_remote_copy(
            src, dst, send.at[k], recv.at[k], device_id=device(mask), device_id_type=MESH
        )

    def arrived(ref, k):
        copy(ref, ref, k, PAIR).wait_recv()
        pending.append((ref, k))

    third = COLS // 3
    ranges = []
    for j in range(3):
        some = pl.ds(j * third, third)
        ranges += [(t_hbm.at[some, :], t_ref.at[some, :]), (p_hbm.at[:, some], p_ref.at[:, some])]
    ranges += [(s_hbm, s_ref), (a_hbm, a_ref), (b_hbm, b_ref), (eps_hbm, eps_ref)]
    loads = [pltpu.make_async_copy(src, dst, load.at[k]) for k, (src, dst) in enumerate(ranges)]
    for one in loads:
        one.start()
    barrier = pltpu.get_barrier_semaphore()
    for mask in GREET:
        pl.semaphore_signal(barrier, inc=1, device_id=device(mask), device_id_type=MESH)

    moved = None
    for j in range(3):
        loads[2 * j].wait()
        loads[2 * j + 1].wait()
        some = slice(j * third, (j + 1) * third)
        th[some], tl[some] = pieces(t_ref[some])
        term = dot(pieces(p_ref[:, some]), (th[some], tl[some]))
        moved = term if moved is None else moved + term
    loads[6].wait()
    sth[...], stl[...] = pieces(s_ref[...].T)
    moved = pieces(moved)
    for k, h in ((0, 1 - core), (1, core)):
        rows = pl.ds(pl.multiple_of(h * HALF, 64), HALF)
        value = dot((sth[rows, :], stl[rows, :]), moved)
        flat = jnp.concatenate([value[:, j * 128 : (j + 1) * 128] for j in range(3)], axis=0)
        for q in range(16):
            half[k, q] = flat[q * SLAB : (q + 1) * SLAB]
        if k == 0:
            pl.semaphore_wait(barrier, len(GREET))
            copy(half.at[0], pair_in, 0, PAIR).start()
    for k in (7, 8, 9):
        loads[k].wait()
    mass = a_ref[...].reshape(1, ROWS)
    target = b_ref[...].reshape(1, COLS)
    adown[...] = jnp.broadcast_to(mass, (128, ROWS)).T
    arrived(pair_in, 0)
    acc[...] = half[1] + pair_in[...]

    for d in NEAR_ORDER:
        copy(acc.at[flipped(g, gb, d)], near_in.at[d - 1], 1, NEAR[d]).start()
    arrived(near_in, 1)
    total = acc[g]
    for d in range(15):
        total = total + near_in[d]
    wide[w] = total

    for d in WIDE_ORDER:
        copy(wide.at[w], wide.at[w], 2, WIDE[d]).start()
    arrived(wide.at[pl.ds(0, 15)], 2)
    total = wide[0]
    for d in range(1, 16):
        total = total + wide[d]
    gathered[core, g] = total / TOTAL

    for d in LATE:
        copy(gathered.at[core, g], gathered.at[core, g], 11, NEAR[d]).start()
    for d in EARLY:
        copy(gathered.at[core, g], gathered.at[core, g], 3, NEAR[d]).start()
    copy(gathered.at[core, g], gathered.at[core, g], 4, PAIR).start()
    for group, k in ((EARLY, 3), (LATE, 11)):
        arrived(gathered.at[0, pl.ds(0, len(group))], k)
        for d in group:
            slab = gathered.at[core, flipped(g, gb, d)]
            copy(slab, slab, 4, PAIR).start()

    def product_of(h):
        rows = pl.ds(pl.multiple_of(h * HALF, 64), HALF)
        flat = jnp.concatenate([gathered[h, q] for q in range(16)], axis=0)
        block = jnp.concatenate([flat[j * HALF : (j + 1) * HALF] for j in range(3)], axis=1)
        core_ref[rows, :] = block
        return dot((sth[rows, :], stl[rows, :]), pieces(block), ((0,), (0,)))

    left = product_of(core)
    arrived(gathered.at[0], 4)
    left = (left + product_of(1 - core)) * (2.0 / eps_ref[0])

    leaving = [
        pltpu.make_async_copy(core_ref, core_hbm, load.at[10]),
        pltpu.make_async_copy(col_ref, col_hbm, load.at[11]),
    ]
    leaving[0].start()

    kern[...] = p_ref[...] * jnp.exp(dot(pieces(left), (th[...], tl[...]), ((1,), (1,))))

    def settle(x):
        x = x + pltpu.roll(x, 4, 0)
        x = x + pltpu.roll(x, 2, 0)
        return x + pltpu.roll(x, 1, 0)

    def row_total(scale, k, n):
        parts = None
        for j in range(COLS // 128):
            piece = kern[:, j * 128 : (j + 1) * 128]
            if scale is not None:
                piece = piece * scale[0:1, j * 128 : (j + 1) * 128]
            parts = piece if parts is None else parts + piece
        across = parts.T
        x = across[0:8]
        for j in range(1, 16):
            x = x + across[j * 8 : (j + 1) * 8]
        row_in[n, 0] = settle(x)[0:1]
        for d in TGT_ORDER:
            copy(row_in.at[n, 0], row_in.at[n, d], k, TGT[d]).start()
        arrived(row_in.at[n, pl.ds(0, 31)], k)
        x = row_in[n, 0]
        for d in range(1, 32):
            x = x + row_in[n, d]
        return x

    def col_total(down, k, n):
        pieces = []
        for j in range(COLS // 128):
            piece = kern[:, j * 128 : (j + 1) * 128] * down
            if n == 1:
                kern[:, j * 128 : (j + 1) * 128] = piece
            x = piece[0:8]
            for i in range(1, 32):
                x = x + piece[i * 8 : (i + 1) * 8]
            pieces.append(settle(x)[0:1])
        col_in[n, si] = jnp.concatenate(pieces, axis=1)
        for d in SRC_ORDER:
            copy(col_in.at[n, si], col_in.at[n, si], k, SRC[d]).start()
        arrived(col_in.at[n, pl.ds(0, 15)], k)
        x = col_in[n, 0]
        for d in range(1, 16):
            x = x + col_in[n, d]
        return x

    scale = None
    for n in range(2):
        row = mass / row_total(scale, 5 + 2 * n, n)
        down = jnp.broadcast_to(row, (128, ROWS)).T
        scale = target / col_total(down, 6 + 2 * n, n)
    col_ref[...] = scale.reshape(COLS)
    leaving[1].start()

    kern4 = kern.reshape(16, 2, 8, COLS)
    for k, h in ((0, 1 - core), (1, core)):
        block = kern4[:, h].reshape(128, COLS) * scale
        part[k] = dot(pieces(block), (th[...], tl[...])).reshape(16, 8, D)
        if k == 0:
            copy(part.at[0], part_in, 9, PAIR).start()
    arrived(part_in, 9)
    mine[...] = part[1] + part_in[...]
    for d in TILE_ORDER:
        copy(mine.at[flipped(tile, tileb, d)], last_in.at[d - 1], 10, TILE[d]).start()
    arrived(last_in, 10)
    total = mine[tile]
    for d in range(15):
        total = total + last_in[d]
    own = adown[pl.ds(pl.multiple_of(ti * 8, 8), 8), :]
    for j in range(D // 128):
        out_ref[:, j * 128 : (j + 1) * 128] = total[:, j * 128 : (j + 1) * 128] / own

    for one in leaving:
        one.wait()
    for ref, k in pending:
        copy(ref, ref, k, PAIR).wait_send()


def leave(out_in, core_in, col_in, out_ref, core_ref, col_ref, sem):
    pairs = [(out_in, out_ref), (col_in, col_ref)]
    for j in range(4):
        rows = pl.ds(j * (D // 4), D // 4)
        pairs.append((core_in.at[rows], core_ref.at[rows]))
    copies = [pltpu.make_async_copy(src, dst, sem.at[k]) for k, (src, dst) in enumerate(pairs)]
    for one in copies:
        one.start()
    for one in copies:
        one.wait()


def per_device(*args):
    f32 = jnp.float32
    vmem = pl.BlockSpec(memory_space=pltpu.VMEM)
    hbm = pl.BlockSpec(memory_space=pltpu.HBM)
    results = (
        jax.ShapeDtypeStruct((8, D), f32),
        jax.ShapeDtypeStruct((D, D), f32),
        jax.ShapeDtypeStruct((COLS,), f32),
    )
    out, core, col = pl.pallas_call(
        body,
        out_shape=results,
        in_specs=[hbm] * 6,
        out_specs=(vmem, hbm, hbm),
        scratch_shapes=[
            pltpu.VMEM((D, D), f32),
            pltpu.VMEM((COLS,), f32),
            pltpu.VMEM((ROWS, D), f32),
            pltpu.VMEM((COLS, D), f32),
            pltpu.VMEM((ROWS, COLS), f32),
            pltpu.VMEM((ROWS,), f32),
            pltpu.VMEM((COLS,), f32),
            pltpu.SMEM((1,), f32),
            pltpu.VMEM((D, ROWS), jnp.bfloat16),
            pltpu.VMEM((D, ROWS), jnp.bfloat16),
            pltpu.VMEM((COLS, D), jnp.bfloat16),
            pltpu.VMEM((COLS, D), jnp.bfloat16),
            pltpu.VMEM((2, 16, SLAB, 128), f32),
            pltpu.VMEM((16, SLAB, 128), f32),
            pltpu.VMEM((16, SLAB, 128), f32),
            pltpu.VMEM((15, SLAB, 128), f32),
            pltpu.VMEM((16, SLAB, 128), f32),
            pltpu.VMEM((2, 16, SLAB, 128), f32),
            pltpu.VMEM((ROWS, COLS), f32),
            pltpu.VMEM((ROWS, 128), f32),
            pltpu.VMEM((2, 32, 1, ROWS), f32),
            pltpu.VMEM((2, 16, 1, COLS), f32),
            pltpu.VMEM((2, 16, 8, D), f32),
            pltpu.VMEM((16, 8, D), f32),
            pltpu.VMEM((16, 8, D), f32),
            pltpu.VMEM((15, 8, D), f32),
            pltpu.SemaphoreType.DMA((12,)),
            pltpu.SemaphoreType.DMA((12,)),
            pltpu.SemaphoreType.DMA((12,)),
        ],
        compiler_params=pltpu.CompilerParams(
            collective_id=0, has_side_effects=True, vmem_limit_bytes=60 * 2**20
        ),
    )(*args)
    out, core, col = pl.pallas_call(
        leave,
        out_shape=results,
        in_specs=[hbm] * 3,
        out_specs=(hbm, hbm, hbm),
        scratch_shapes=[pltpu.SemaphoreType.DMA((6,))],
        compiler_params=pltpu.CompilerParams(vmem_limit_bytes=60 * 2**20),
    )(out, core, col)
    return out, core, col


def solution(mesh):
    return jax.shard_map(
        per_device,
        mesh=mesh,
        in_specs=(P("src", None), P("tgt", None), P("src", "tgt"), P("src"), P("tgt"), P()),
        out_specs=(P(("src", "tgt"), None), P(), P("tgt")),
        check_vma=False,
    )
```

time: 90.3 us -> 95.8 us (1.061)
  Pallas kernels: 81 us -> 94.3 us
  local copies, waits for them, and re-layouts: 6.33 us -> 0 us
  other arithmetic: 1.28 us -> 0 us
    pallas_call x1 -> x2, Pallas kernels: 81 us -> 94.3 us  [the longest x1 74.9 us: per_device(): pl.pallas_call(body, out_shape=results, in_specs=[hbm] * 6, out_specs=(vm...]
    unnamed x9 -> x0, local copies, waits for them, and re-layouts: 4.89 us -> none
where the time goes in v4:
time: 95.8 us; the launch traced here: 95.6 us
  Pallas kernels  94.3 us (98%)
  between operations  1.29 us (1%)
    pallas_call x1, Pallas kernels, per_device(): pl.pallas_call(body, out_shape=results, in_specs=[hbm] * 6, out_specs=(vm...  74.9 us
    pallas_call x1, Pallas kernels, per_device(): pl.pallas_call(leave, out_shape=results, in_specs=[hbm] * 3, out_specs=(h...  19.5 us

profile of v4, /device:TPU:1, one launch (start us, length us, event | category | flops | bytes accessed | tf_op | source)
XLA Modules:
  0.0 95.6 jit_solution(13222846581457165572)
XLA Ops:
  1.3 74.9 %shard_map.85 = (f32[8,384]{1,0:T(8,128)}, f32[384,384]{1,0:T(8,128)}, f32[768]{0:T(1024)}) custom-call(f32[256,384]{1,0:T(8,128)} %s_hbm.1, f32[768,384]{1,0:T(8,128)} %t_hbm.1, f32[256,768]{1,0:T(8,128)} %p_hbm.1, f32[256]{0:T(256)} %a_hbm.1, f32[768]{0:T(1024)} %b_hbm.1, f32[1]{0:T(128)S(6)} %copy.9.eps_hbm), custom_call_target="tpu_custom_call" | custom-call | tf_op jit(solution)/shard_map/pallas_call | solution.py:297
  76.1 19.5 %shard_map.86 = (f32[8,384]{1,0:T(8,128)}, f32[384,384]{1,0:T(8,128)}, f32[768]{0:T(1024)}) custom-call(f32[8,384]{1,0:T(8,128)} %get-tuple-element.6.out_in, f32[384,384]{1,0:T(8,128)} %get-tuple-element.7.core_in, f32[768]{0:T(1024)} %get-tuple-element.8.col_in), custom_call_target="tpu_custom_call" | custom-call | tf_op jit(solution)/shard_map/pallas_call | solution.py:337

commit v5 on v4

--- a/solution.py
+++ b/solution.py
@@ -83,8 +83,8 @@
 
 def body(
     s_hbm, t_hbm, p_hbm, a_hbm, b_hbm, eps_hbm,
-    out_ref, core_hbm, col_hbm,
-    core_ref, col_ref, s_ref, t_ref, p_ref, a_ref, b_ref, eps_ref,
+    out_ref, core_ref, col_ref,
+    s_ref, t_ref, p_ref, a_ref, b_ref, eps_ref,
     sth, stl, th, tl, half, pair_in, acc, near_in, wide, gathered, kern, adown, row_in, col_in, part, part_in, mine, last_in,
     load, send, recv,
 ):
@@ -189,12 +189,6 @@
     arrived(gathered.at[0], 4)
     left = (left + product_of(1 - core)) * (2.0 / eps_ref[0])
 
-    leaving = [
-        pltpu.make_async_copy(core_ref, core_hbm, load.at[10]),
-        pltpu.make_async_copy(col_ref, col_hbm, load.at[11]),
-    ]
-    leaving[0].start()
-
     kern[...] = p_ref[...] * jnp.exp(dot(pieces(left), (th[...], tl[...]), ((1,), (1,))))
 
     def settle(x):
@@ -247,7 +241,6 @@
         down = jnp.broadcast_to(row, (128, ROWS)).T
         scale = target / col_total(down, 6 + 2 * n, n)
     col_ref[...] = scale.reshape(COLS)
-    leaving[1].start()
 
     kern4 = kern.reshape(16, 2, 8, COLS)
     for k, h in ((0, 1 - core), (1, core)):
@@ -267,17 +260,12 @@
     for j in range(D // 128):
         out_ref[:, j * 128 : (j + 1) * 128] = total[:, j * 128 : (j + 1) * 128] / own
 
-    for one in leaving:
-        one.wait()
     for ref, k in pending:
         copy(ref, ref, k, PAIR).wait_send()
 
 
 def leave(out_in, core_in, col_in, out_ref, core_ref, col_ref, sem):
-    pairs = [(out_in, out_ref), (col_in, col_ref)]
-    for j in range(4):
-        rows = pl.ds(j * (D // 4), D // 4)
-        pairs.append((core_in.at[rows], core_ref.at[rows]))
+    pairs = ((core_in, core_ref), (out_in, out_ref), (col_in, col_ref))
     copies = [pltpu.make_async_copy(src, dst, sem.at[k]) for k, (src, dst) in enumerate(pairs)]
     for one in copies:
         one.start()
@@ -298,10 +286,8 @@
         body,
         out_shape=results,
         in_specs=[hbm] * 6,
-        out_specs=(vmem, hbm, hbm),
+        out_specs=(vmem, vmem, vmem),
         scratch_shapes=[
-            pltpu.VMEM((D, D), f32),
-            pltpu.VMEM((COLS,), f32),
             pltpu.VMEM((ROWS, D), f32),
             pltpu.VMEM((COLS, D), f32),
             pltpu.VMEM((ROWS, COLS), f32),
@@ -326,21 +312,21 @@
             pltpu.VMEM((16, 8, D), f32),
             pltpu.VMEM((16, 8, D), f32),
             pltpu.VMEM((15, 8, D), f32),
-            pltpu.SemaphoreType.DMA((12,)),
+            pltpu.SemaphoreType.DMA((10,)),
             pltpu.SemaphoreType.DMA((12,)),
             pltpu.SemaphoreType.DMA((12,)),
         ],
         compiler_params=pltpu.CompilerParams(
-            collective_id=0, has_side_effects=True, vmem_limit_bytes=60 * 2**20
+            collective_id=0, has_side_effects=True, vmem_limit_bytes=40 * 2**20
         ),
-    )(*args)
+    )(*[pltpu.with_memory_space_constraint(x, pltpu.HBM) for x in args[:5]], args[5])
     out, core, col = pl.pallas_call(
         leave,
         out_shape=results,
-        in_specs=[hbm] * 3,
+        in_specs=[vmem] * 3,
         out_specs=(hbm, hbm, hbm),
-        scratch_shapes=[pltpu.SemaphoreType.DMA((6,))],
-        compiler_params=pltpu.CompilerParams(vmem_limit_bytes=60 * 2**20),
+        scratch_shapes=[pltpu.SemaphoreType.DMA((3,))],
+        compiler_params=pltpu.CompilerParams(vmem_limit_bytes=2**20),
     )(out, core, col)
     return out, core, col
 

time: 95.8 us -> 76.5 us (0.80)
  Pallas kernels: 94.3 us -> 75.1 us
    pallas_call x1, Pallas kernels: 19.5 us -> 0.85 us  [per_device(): pl.pallas_call(leave, out_shape=results, in_specs=[vmem] * 3, out_specs=(...]
where the time goes in v5:
time: 76.5 us; the launch traced here: 76.4 us
  Pallas kernels  75.1 us (98%)
  between operations  1.29 us (2%)
    pallas_call x1, Pallas kernels, per_device(): pl.pallas_call(body, out_shape=results, in_specs=[hbm] * 6, out_specs=(vm...  74.2 us

profile of v5, /device:TPU:1, one launch (start us, length us, event | category | flops | bytes accessed | tf_op | source)
XLA Modules:
  0.0 76.4 jit_solution(7138853676177466241)
XLA Ops:
  1.3 74.2 %shard_map.85 = (f32[8,384]{1,0:T(8,128)S(1)}, f32[384,384]{1,0:T(8,128)S(1)}, f32[768]{0:T(1024)S(1)}) custom-call(f32[256,384]{1,0:T(8,128)} %s_hbm.1, f32[768,384]{1,0:T(8,128)} %t_hbm.1, f32[256,768]{1,0:T(8,128)} %p_hbm.1, f32[256]{0:T(256)} %a_hbm.1, f32[768]{0:T(1024)} %b_hbm.1, f32[1]{0:T(128)S(6)} %copy.9.eps_hbm), custom_call_target="tpu_custom_call" | custom-call | tf_op jit(solution)/shard_map/pallas_call | solution.py:285
  75.5 0.8 %shard_map.86 = (f32[8,384]{1,0:T(8,128)}, f32[384,384]{1,0:T(8,128)}, f32[768]{0:T(1024)}) custom-call(f32[8,384]{1,0:T(8,128)S(1)} %get-tuple-element.6.out_in, f32[384,384]{1,0:T(8,128)S(1)} %get-tuple-element.7.core_in, f32[768]{0:T(1024)S(1)} %get-tuple-element.8.col_in), custom_call_target="tpu_custom_call" | custom-call | tf_op jit(solution)/shard_map/pallas_call | solution.py:323

commit v6 on v5

--- a/solution.py
+++ b/solution.py
@@ -111,11 +111,11 @@
         pending.append((ref, k))
 
     third = COLS // 3
-    ranges = []
+    ranges = [(s_hbm, s_ref)]
     for j in range(3):
         some = pl.ds(j * third, third)
         ranges += [(t_hbm.at[some, :], t_ref.at[some, :]), (p_hbm.at[:, some], p_ref.at[:, some])]
-    ranges += [(s_hbm, s_ref), (a_hbm, a_ref), (b_hbm, b_ref), (eps_hbm, eps_ref)]
+    ranges += [(a_hbm, a_ref), (b_hbm, b_ref), (eps_hbm, eps_ref)]
     loads = [pltpu.make_async_copy(src, dst, load.at[k]) for k, (src, dst) in enumerate(ranges)]
     for one in loads:
         one.start()
@@ -123,16 +123,16 @@
     for mask in GREET:
         pl.semaphore_signal(barrier, inc=1, device_id=device(mask), device_id_type=MESH)
 
+    loads[0].wait()
+    sth[...], stl[...] = pieces(s_ref[...].T)
     moved = None
     for j in range(3):
-        loads[2 * j].wait()
         loads[2 * j + 1].wait()
+        loads[2 * j + 2].wait()
         some = slice(j * third, (j + 1) * third)
         th[some], tl[some] = pieces(t_ref[some])
         term = dot(pieces(p_ref[:, some]), (th[some], tl[some]))
         moved = term if moved is None else moved + term
-    loads[6].wait()
-    sth[...], stl[...] = pieces(s_ref[...].T)
     moved = pieces(moved)
     for k, h in ((0, 1 - core), (1, core)):
         rows = pl.ds(pl.multiple_of(h * HALF, 64), HALF)
@@ -220,8 +220,6 @@
         pieces = []
         for j in range(COLS // 128):
             piece = kern[:, j * 128 : (j + 1) * 128] * down
-            if n == 1:
-                kern[:, j * 128 : (j + 1) * 128] = piece
             x = piece[0:8]
             for i in range(1, 32):
                 x = x + piece[i * 8 : (i + 1) * 8]
@@ -229,6 +227,9 @@
         col_in[n, si] = jnp.concatenate(pieces, axis=1)
         for d in SRC_ORDER:
             copy(col_in.at[n, si], col_in.at[n, si], k, SRC[d]).start()
+        if n == 1:
+            for j in range(COLS // 128):
+                kern[:, j * 128 : (j + 1) * 128] = kern[:, j * 128 : (j + 1) * 128] * down
         arrived(col_in.at[n, pl.ds(0, 15)], k)
         x = col_in[n, 0]
         for d in range(1, 16):

time: 76.5 us -> 76.5 us (level)
  no operation moved by 1% of the time
where the time goes in v6:
time: 76.5 us; the launch traced here: 76.4 us
  Pallas kernels  75.1 us (98%)
  between operations  1.29 us (2%)
    pallas_call x1, Pallas kernels, per_device(): pl.pallas_call(body, out_shape=results, in_specs=[hbm] * 6, out_specs=(vm...  74.2 us

profile of v6, /device:TPU:1, one launch (start us, length us, event | category | flops | bytes accessed | tf_op | source)
XLA Modules:
  0.0 76.4 jit_solution(9451175074547534728)
XLA Ops:
  1.3 74.2 %shard_map.85 = (f32[8,384]{1,0:T(8,128)S(1)}, f32[384,384]{1,0:T(8,128)S(1)}, f32[768]{0:T(1024)S(1)}) custom-call(f32[256,384]{1,0:T(8,128)} %s_hbm.1, f32[768,384]{1,0:T(8,128)} %t_hbm.1, f32[256,768]{1,0:T(8,128)} %p_hbm.1, f32[256]{0:T(256)} %a_hbm.1, f32[768]{0:T(1024)} %b_hbm.1, f32[1]{0:T(128)S(6)} %copy.9.eps_hbm), custom_call_target="tpu_custom_call" | custom-call | tf_op jit(solution)/shard_map/pallas_call | solution.py:286
  75.5 0.8 %shard_map.86 = (f32[8,384]{1,0:T(8,128)}, f32[384,384]{1,0:T(8,128)}, f32[768]{0:T(1024)}) custom-call(f32[8,384]{1,0:T(8,128)S(1)} %get-tuple-element.6.out_in, f32[384,384]{1,0:T(8,128)S(1)} %get-tuple-element.7.core_in, f32[768]{0:T(1024)S(1)} %get-tuple-element.8.col_in), custom_call_target="tpu_custom_call" | custom-call | tf_op jit(solution)/shard_map/pallas_call | solution.py:324
